TPU v7x, 256 devices: a whole 4x4x8 slice. The times are simulated.
256 devices in a mesh: comp: 16 (over x_lo, z), shard: 16 (over y, x_hi, core).
Axes of the slice: x: 4 (x_hi: 2, x_lo: 2; x = x_hi * 2 + x_lo), y: 4, z: 8, core: 2. Of those that a mesh axis runs over, the one named last changes fastest.
Arguments:
- modal_coefs: float32 [16, 16, 512, 256], P('comp', 'shard'), may hold values from -6 to 6
- comp_levels: int32 [16, 3], replicated, may hold values from 2 to 5, as said below
- comp_coefs: int32 [16], replicated, may hold values from -2 to 2, as said below
- velocity: float32 [4], replicated, may hold values from 0.5 to 2
Outputs:
- combined: float32 [16, 16, 512, 256], P('comp', 'shard')
Inputs may be any that keep to these rules, and one draw needn't show every extreme that they name: `comp_levels`: each row sums to 9. `comp_coefs`: never zero.
All inputs are finite; a program needn't handle non-finite values.
Results may differ from a plain program's by a relative error of at most 0.0003.
Values sent between devices are 32-bit elements; how exact they have to be, the bound alone decides.
A program may use at most 64 MiB of HBM per device.

v0:
```python
import functools

import jax
import jax.numpy as jnp
import ml_dtypes
import numpy as np
from jax import lax
from jax.experimental import pallas as pl
from jax.experimental.pallas import tpu as pltpu
from jax.sharding import PartitionSpec as P

COEF = 256
BASE = 2
RISE = 3
GRID = 512
LOW = 2**RISE
PLACES = (2**BASE) ** 3
KINDS = (RISE + 1) * (RISE + 2) // 2
BF16 = jnp.bfloat16
F32 = jnp.float32
MESH = pl.DeviceIdType.MESH

courant = 0.1


def legendre(order, points):
    values = np.asarray(points) * 1.0
    if order == 0:
        poly = values * 0.0 + 1.0
    elif order == 1:
        poly = values
    elif order == 2:
        poly = (3.0 * values * values - 1.0) / 2.0
    else:
        poly = (5.0 * values * values * values - 3.0 * values) / 2.0
    return np.sqrt((2 * order + 1) / 2.0) * poly


def line_tables():
    nodes = np.array(
        [-0.8611363115940526, -0.3399810435848563, 0.3399810435848563, 0.8611363115940526]
    )
    weights = np.array(
        [0.3478548451374538, 0.6521451548625461, 0.6521451548625461, 0.3478548451374538]
    )
    stiff = np.zeros((4, 4))
    coarse = np.zeros((4, 8))
    for row in range(4):
        for column in range(4):
            if column < row and (row + column) % 2 == 1:
                stiff[row, column] = np.sqrt((2.0 * row + 1.0) * (2.0 * column + 1.0))
            coarse[row, column] = np.sum(
                weights * legendre(row, (nodes - 1.0) / 2.0) * legendre(column, nodes)
            ) / np.sqrt(2.0)
            coarse[row, column + 4] = np.sum(
                weights * legendre(row, (nodes + 1.0) / 2.0) * legendre(column, nodes)
            ) / np.sqrt(2.0)
    right = np.array([float(legendre(order, 1.0)) for order in range(4)])
    left = np.array([float(legendre(order, -1.0)) for order in range(4)])
    rows = [coarse[index] for index in range(4)]
    for index in range(4, 8):
        vector = np.eye(8)[index]
        for other in rows:
            vector = vector - np.dot(other, vector) * other
        rows.append(vector / np.sqrt(np.sum(vector * vector)))
    return (stiff - np.outer(right, right), right, left, np.array(rows))


def along(matrix, axis):
    return np.kron(np.eye(4**axis), np.kron(matrix, np.eye(4 ** (3 - axis))))


def split_table(table):
    hi = table.astype(ml_dtypes.bfloat16)
    lo = (table - hi.astype(np.float64)).astype(ml_dtypes.bfloat16)
    return np.stack([hi, lo], axis=-3)


def line_hierarchy(filters, rise):
    cells = 2**rise
    whole = np.eye(cells * 4).reshape(cells, 4, cells * 4)
    for level_step in range(rise):
        for first in range(0, cells, 2 ** (level_step + 1)):
            second = first + 2**level_step
            pair = np.concatenate([whole[first], whole[second]], axis=0)
            mixed = filters @ pair
            whole[first], whole[second] = mixed[:4], mixed[4:]
    ordered = np.zeros_like(whole)
    for low in range(cells):
        digit = 0
        if low > 0:
            zeros = (low & -low).bit_length() - 1
            height = rise - zeros
            digit = 2 ** (height - 1) + (low >> (zeros + 1))
        ordered[digit] = whole[low]
    return ordered.reshape(cells, 4, cells, 4)


def compositions():
    return [(a, b, RISE - a - b) for a in range(RISE + 1) for b in range(RISE + 1 - a)]


@functools.lru_cache(None)
def tables():
    interior, right, left, filters = line_tables()
    stiff = np.stack([along(interior, axis).T for axis in range(4)]).astype(np.float32)
    lift = np.concatenate([along(left[:, None], axis).T for axis in range(4)]).astype(np.float32)
    trace = np.concatenate([along(right[None, :], axis) for axis in range(4)], axis=0).T
    lines = [line_hierarchy(filters, rise) for rise in range(RISE + 1)]
    hier = []
    for one, two, three in compositions():
        whole = np.einsum("aqlp,brms,cuno->qruabclmnpso", lines[one], lines[two], lines[three])
        hier.append(whole.reshape(GRID, GRID))
    return stiff, lift, split_table(trace), split_table(np.stack(hier))


def split(values):
    hi = values.astype(BF16)
    return hi, (values - hi.astype(F32)).astype(BF16)


def dot(one, two):
    return jnp.dot(one, two, preferred_element_type=F32)


def dot_nt(one, two):
    return lax.dot_general(one, two, (((1,), (1,)), ((), ())), preferred_element_type=F32)


def kernel(
    comps,
    shards,
    levels,
    coefs,
    velocity,
    x_hbm,
    stiff_hbm,
    lift_hbm,
    trace_hbm,
    hier_hbm,
    out_hbm,
    x_v,
    stiff_v,
    lift_v,
    trace_v,
    hier_v,
    onehot,
    match,
    wide,
    lifts,
    field,
    traces1,
    traces2,
    shifted,
    section,
    edge_out,
    edge_in,
    rows,
    sent,
    got,
    back,
    home,
    local_sem,
    edge_send,
    edge_recv,
    there_send,
    there_recv,
    back_send,
    back_recv,
):
    me = lax.axis_index("comp")
    spot = lax.axis_index("shard")
    ahead = lax.rem(spot + 1, shards)
    behind = lax.rem(spot + shards - 1, shards)

    x_copy = pltpu.make_async_copy(x_hbm.at[0, 0], x_v, local_sem.at[0])
    trace_copy = pltpu.make_async_copy(trace_hbm, trace_v, local_sem.at[1])
    stiff_copy = pltpu.make_async_copy(stiff_hbm, stiff_v, local_sem.at[2])
    lift_copy = pltpu.make_async_copy(lift_hbm, lift_v, local_sem.at[3])
    hier_copy = pltpu.make_async_copy(hier_hbm, hier_v, local_sem.at[4])
    x_copy.start()
    stiff_copy.start()
    lift_copy.start()
    trace_copy.start()
    hier_copy.start()

    barrier = pltpu.get_barrier_semaphore()
    others = [lax.rem(me + step, comps) for step in range(1, comps)]
    for other in others:
        pl.semaphore_signal(barrier, inc=1, device_id={"comp": other}, device_id_type=MESH)
    pl.semaphore_signal(barrier, inc=1, device_id={"shard": ahead}, device_id_type=MESH)
    pl.semaphore_signal(barrier, inc=1, device_id={"shard": behind}, device_id_type=MESH)

    def rise_of(comp, axis):
        return jnp.clip(levels[comp, axis] - BASE, 0, RISE)

    rise1 = rise_of(me, 0)
    rise2 = rise_of(me, 1)
    rise3 = rise_of(me, 2)
    kind = jnp.clip(lax.shift_right_logical(rise1 * (9 - rise1), 1) + rise2, 0, KINDS - 1)
    one = jnp.int32(1)
    reach = None
    for comp in range(comps):
        total = velocity[0] * (1.0 * shards)
        for axis in range(3):
            size = lax.shift_left(one, levels[comp, axis]).astype(F32)
            total = total + velocity[axis + 1] * size
        reach = total if reach is None else jnp.maximum(reach, total)
    step_size = jnp.full((1, COEF), courant, F32) / jnp.full((1, COEF), reach, F32)
    sizes = [jnp.float32(shards)] + [
        lax.shift_left(one, levels[me, axis]).astype(F32) for axis in range(3)
    ]
    scales = [step_size * (2.0 * velocity[axis] * sizes[axis]) for axis in range(4)]

    def low_digits(low):
        low3 = low & (lax.shift_left(one, rise3) - 1)
        low2 = lax.shift_right_logical(low, rise3) & (lax.shift_left(one, rise2) - 1)
        low1 = lax.shift_right_logical(low, rise2 + rise3)
        return low1, low2, low3

    def cell_of(digit1, digit2, digit3):
        return (
            lax.shift_left(digit1, rise2 + rise3 + 2 * BASE)
            + lax.shift_left(digit2, rise3 + BASE)
            + digit3
        )

    offsets = [cell_of(*low_digits(jnp.int32(low))) for low in range(LOW)]

    def place_cell(place):
        return cell_of(
            lax.shift_left(lax.shift_right_logical(place, 4) & 3, jnp.full(place.shape, rise1)),
            lax.shift_left(lax.shift_right_logical(place, 2) & 3, jnp.full(place.shape, rise2)),
            lax.shift_left(place & 3, jnp.full(place.shape, rise3)),
        )

    place_rows = place_cell(lax.broadcasted_iota(jnp.int32, (PLACES, 128), 0))
    lanes = lax.broadcasted_iota(jnp.int32, (PLACES, 128), 1)
    for low in range(LOW):
        for part in range(GRID // 128):
            hit = (place_rows + offsets[low]) == (lanes + 128 * part)
            onehot[low * PLACES : (low + 1) * PLACES, 128 * part : 128 * (part + 1)] = jnp.where(
                hit, 1.0, 0.0
            ).astype(BF16)

    stiff_copy.wait()
    volume = scales[0] * stiff_v[0]
    for axis in range(1, 4):
        volume = volume + scales[axis] * stiff_v[axis]
    wide[0], wide[1] = split(volume)
    lift_copy.wait()
    for axis in range(4):
        rows_of = slice(64 * axis, 64 * (axis + 1))
        hi, lo = split(scales[axis] * lift_v[rows_of, :])
        lifts[0, rows_of, :] = hi
        lifts[1, rows_of, :] = lo

    x_copy.wait()
    hi, lo = split(x_v[...])
    field[...] = dot(onehot[...], hi) + dot(onehot[...], lo)

    left_half = lax.broadcasted_iota(jnp.int32, (PLACES, 128), 1) < 64
    place_row = lax.broadcasted_iota(jnp.int32, (PLACES, 128), 0)

    def halves(one, two):
        return jnp.where(left_half, one, two)

    def swap(values):
        return pltpu.roll(values, 64, 1)

    def behind_of(low, axis):
        digits = list(low_digits(jnp.int32(low)))
        rise = (rise1, rise2, rise3)[axis]
        first = digits[axis] == 0
        digits[axis] = (digits[axis] + lax.shift_left(one, rise) - 1) & (
            lax.shift_left(one, rise) - 1
        )
        spot = (
            lax.shift_left(digits[0], rise2 + rise3) + lax.shift_left(digits[1], rise3) + digits[2]
        )
        return spot & (LOW - 1), first

    sources = []
    for low in range(LOW):
        spot1, first1 = behind_of(low, 0)
        spot2, first2 = behind_of(low, 1)
        spot3, first3 = behind_of(low, 2)
        sources.append(
            (
                spot1 + jnp.where(first1, LOW, 0),
                spot2 + jnp.where(first2, LOW, 0),
                spot3 + jnp.where(first3, 2 * LOW, 0),
            )
        )

    trace_copy.wait()

    def slope_step(hi, lo, stage, after_start):
        trace = (
            dot(hi, trace_v[0]) + dot(lo, trace_v[0]) + dot(hi, trace_v[1])
        ).reshape(LOW, PLACES, COEF)
        t01, t23 = trace[:, :, :128], trace[:, :, 128:]
        for low in range(LOW // 2):
            edge_out[stage, low] = halves(t01[low], swap(t01[low + LOW // 2]))
        after_start()
        copy = pltpu.make_async_remote_copy(
            src_ref=edge_out.at[stage],
            dst_ref=edge_in.at[stage],
            send_sem=edge_send.at[stage],
            recv_sem=edge_recv.at[stage],
            device_id={"shard": ahead},
            device_id_type=MESH,
        )
        copy.start()
        for low in range(LOW):
            traces1[low] = t01[low]
            traces1[LOW + low] = pltpu.roll(t01[low], 16, 0)
            now = t23[low]
            traces2[low] = now
            traces2[LOW + low] = jnp.where(
                (place_row & 15) < 4, pltpu.roll(now, PLACES - 12, 0), pltpu.roll(now, 4, 0)
            )
            traces2[2 * LOW + low] = jnp.where(
                (place_row & 3) < 1, pltpu.roll(now, PLACES - 3, 0), pltpu.roll(now, 1, 0)
            )
        inner = dot(hi, wide[0]) + dot(lo, wide[0]) + dot(hi, wide[1])
        copy.wait()
        for low in range(LOW):
            edge = edge_in[stage, low % (LOW // 2)]
            if low >= LOW // 2:
                edge = swap(edge)
            from1, from2, from3 = sources[low]
            rows_of = slice(low * PLACES, (low + 1) * PLACES)
            shifted[rows_of, :128] = halves(edge, traces1[from1])
            shifted[rows_of, 128:] = halves(traces2[from2], traces2[from3])
        s_hi, s_lo = split(shifted[...])
        return inner + (dot(s_hi, lifts[0]) + dot(s_lo, lifts[0]) + dot(s_hi, lifts[1]))

    def wait_barrier():
        pl.semaphore_wait(barrier, comps + 1)

    hi, lo = split(field[...])
    section[...] = field[...] + slope_step(hi, lo, 0, wait_barrier)
    hi, lo = split(section[...])
    section[...] = 0.5 * field[...] + 0.5 * (
        section[...] + slope_step(hi, lo, 1, lambda: None)
    )

    for pair in range(LOW // 2):
        for group in range(2):
            columns = slice(128 * group, 128 * (group + 1))
            even = section[2 * pair * PLACES : (2 * pair + 1) * PLACES, columns]
            odd = section[(2 * pair + 1) * PLACES : (2 * pair + 2) * PLACES, columns]
            for half, block in ((0, halves(even, swap(odd))), (1, halves(swap(even), odd))):
                top = (2 * group + half) * PLACES
                hi, lo = split(block)
                rows[0, top : top + PLACES, 128 * pair : 128 * (pair + 1)] = hi
                rows[1, top : top + PLACES, 128 * pair : 128 * (pair + 1)] = lo

    hier_copy.wait()
    h_hi, h_lo = hier_v[kind, 0], hier_v[kind, 1]
    hier = dot_nt(h_hi, rows[0]) + dot_nt(h_hi, rows[1]) + dot_nt(h_lo, rows[0])
    sent[...] = hier.reshape(sent.shape)

    def exchange(source, target, send_sem, recv_sem):
        copies = []
        for step in (8, 4, 12, 5, 11, 3, 13, 6, 10, 2, 14, 7, 9, 1, 15):
            other = lax.rem(me + step, comps)
            copy = pltpu.make_async_remote_copy(
                src_ref=source.at[other],
                dst_ref=target.at[me],
                send_sem=send_sem.at[step],
                recv_sem=recv_sem.at[step],
                device_id={"comp": other},
                device_id_type=MESH,
            )
            copy.start()
            copies.append(copy)
        target[me] = source[me]
        return copies

    copies = exchange(sent, got, there_send, there_recv)

    def code_of(digits, comp):
        up2 = rise_of(comp, 1)
        up3 = rise_of(comp, 2)
        digit3 = digits & (lax.shift_left(one, up3) - 1)
        digit2 = lax.shift_right_logical(digits, jnp.full(digits.shape, up3)) & (
            lax.shift_left(one, up2) - 1
        )
        digit1 = lax.shift_right_logical(digits, jnp.full(digits.shape, up2 + up3))
        return digit1 * 64 + digit2 * 8 + digit3

    piece_row = lax.broadcasted_iota(jnp.int32, (8, 128), 0)
    piece_lane = lax.broadcasted_iota(jnp.int32, (8, 128), 1)
    lane_code = jnp.zeros((8, 128), jnp.int32)
    lane_coef = jnp.zeros((8, 128), F32)
    for comp in range(comps):
        own = lax.shift_right_logical(piece_lane, 3) == comp
        lane_code = jnp.where(own, code_of(piece_lane & 7, comp), lane_code)
        lane_coef = jnp.where(own, jnp.full((8, 128), coefs[comp].astype(F32)), lane_coef)
    for comp in range(0, comps, 2):
        block = [
            jnp.where(code_of(piece_row, here) == lane_code, lane_coef, 0.0)
            for here in (comp, comp + 1)
        ]
        match[8 * comp : 8 * comp + 16, :] = jnp.concatenate(block, axis=0).astype(BF16)

    for copy in copies:
        copy.wait()
    for quarter in range(4):
        part = slice(8 * quarter, 8 * (quarter + 1))
        hi, lo = split(got[:, part, :].reshape(8 * comps, COEF))
        total = dot(match[...], hi) + dot(match[...], lo)
        back[:, part, :] = total.reshape(comps, 8, COEF)
    copies = exchange(back, home, back_send, back_recv)

    cell_rows = lax.broadcasted_iota(jnp.int32, (GRID, 128), 0)
    lane = lax.broadcasted_iota(jnp.int32, (8, 128), 1)
    lane_place = place_cell(lane & (PLACES - 1))
    for part in range(GRID // 128):
        lane_cell = lane_place + jnp.where(lane < 64, offsets[2 * part], offsets[2 * part + 1])
        onehot[:, 128 * part : 128 * (part + 1)] = jnp.where(
            cell_rows == lane_cell[0:1, :], 1.0, 0.0
        ).astype(BF16)

    for copy in copies:
        copy.wait()
    hi, lo = split(home[...].reshape(GRID, COEF).T)
    plain = dot(hi, h_hi) + dot(lo, h_hi) + dot(hi, h_lo)
    for pair in range(LOW // 2):
        for group in range(2):
            columns = slice(128 * group, 128 * (group + 1))
            one_block = plain[
                2 * group * PLACES : (2 * group + 1) * PLACES, 128 * pair : 128 * (pair + 1)
            ]
            two_block = plain[
                (2 * group + 1) * PLACES : (2 * group + 2) * PLACES, 128 * pair : 128 * (pair + 1)
            ]
            section[2 * pair * PLACES : (2 * pair + 1) * PLACES, columns] = halves(
                one_block, swap(two_block)
            )
            section[(2 * pair + 1) * PLACES : (2 * pair + 2) * PLACES, columns] = halves(
                swap(one_block), two_block
            )
    hi, lo = split(section[...])
    x_v[...] = dot(onehot[...], hi) + dot(onehot[...], lo)
    out_copy = pltpu.make_async_copy(x_v, out_hbm.at[0, 0], local_sem.at[0])
    out_copy.start()
    out_copy.wait()


def on_device(modal_coefs, comp_levels, comp_coefs, velocity):
    comps = lax.axis_size("comp")
    shards = lax.axis_size("shard")
    stiff, lift, trace, hier = tables()
    smem = pl.BlockSpec(memory_space=pltpu.SMEM)
    anywhere = pl.BlockSpec(memory_space=pl.ANY)
    dma = pltpu.SemaphoreType.DMA
    exchanged = pltpu.VMEM((comps, GRID // comps, COEF), F32)
    return pl.pallas_call(
        functools.partial(kernel, comps, shards),
        out_shape=jax.ShapeDtypeStruct(modal_coefs.shape, F32),
        in_specs=[smem] * 3 + [anywhere] * 5,
        out_specs=anywhere,
        scratch_shapes=[
            pltpu.VMEM((GRID, COEF), F32),
            pltpu.VMEM(stiff.shape, F32),
            pltpu.VMEM(lift.shape, F32),
            pltpu.VMEM(trace.shape, BF16),
            pltpu.VMEM(hier.shape, BF16),
            pltpu.VMEM((GRID, GRID), BF16),
            pltpu.VMEM((8 * comps, 8 * comps), BF16),
            pltpu.VMEM((2, COEF, COEF), BF16),
            pltpu.VMEM((2, COEF, COEF), BF16),
            pltpu.VMEM((GRID, COEF), F32),
            pltpu.VMEM((2 * LOW, PLACES, 128), F32),
            pltpu.VMEM((3 * LOW, PLACES, 128), F32),
            pltpu.VMEM((GRID, COEF), F32),
            pltpu.VMEM((GRID, COEF), F32),
            pltpu.VMEM((2, LOW // 2, PLACES, 128), F32),
            pltpu.VMEM((2, LOW // 2, PLACES, 128), F32),
            pltpu.VMEM((2, COEF, GRID), BF16),
            exchanged,
            exchanged,
            exchanged,
            exchanged,
            dma((5,)),
            dma((2,)),
            dma((2,)),
            dma((comps,)),
            dma((comps,)),
            dma((comps,)),
            dma((comps,)),
        ],
        compiler_params=pltpu.CompilerParams(
            collective_id=0, has_side_effects=True, vmem_limit_bytes=48 * 2**20
        ),
        name="combine",
    )(
        comp_levels,
        comp_coefs,
        velocity,
        modal_coefs,
        jnp.asarray(stiff),
        jnp.asarray(lift),
        jnp.asarray(trace),
        jnp.asarray(hier),
    )


def solution(mesh):
    placed = (P("comp", "shard", None, None), P(), P(), P())
    return jax.shard_map(
        on_device,
        mesh=mesh,
        in_specs=placed,
        out_specs=P("comp", "shard", None, None),
        check_vma=False,
    )
```

profile of v0, /device:TPU:1, one launch (start us, length us, event | category | flops | bytes accessed | tf_op | source)
XLA Modules:
  0.0 57.5 jit_solution(8547084247789758792)
XLA Ops:
  0.0 0.8 %copy.9.levels = s32[16,3]{1,0:T(8,128)S(1)} copy(s32[16,3]{0,1:T(4,128)} %param.9) | data formatting | bytes 384 | tf_op args[1]
  0.8 0.0 copy-start
  0.8 1.2 %copy-done = f32[4,256,256]{2,1,0:T(8,128)S(1)} copy-done((f32[4,256,256]{2,1,0:T(8,128)S(1)}, f32[4,256,256]{2,1,0:T(8,128)}, u32[]{:S(2)}) %copy-start) | copy-done | bytes 1048600
  2.0 0.0 copy-start.1
  2.0 1.0 %copy-done.1 = f32[1,1,512,256]{3,2,1,0:T(8,128)S(1)} copy-done((f32[1,1,512,256]{3,2,1,0:T(8,128)S(1)}, f32[1,1,512,256]{3,2,1,0:T(8,128)}, u32[]{:S(2)}) %copy-start.1) | copy-done | bytes 524312
  3.0 0.0 copy-start.2
  3.0 0.9 %copy-done.2 = bf16[2,256,256]{2,1,0:T(8,128)(2,1)S(1)} copy-done((bf16[2,256,256]{2,1,0:T(8,128)(2,1)S(1)}, bf16[2,256,256]{2,1,0:T(8,128)(2,1)}, u32[]{:S(2)}) %copy-start.2) | copy-done | bytes 262168
  4.0 0.0 copy-start.3
  4.0 0.9 %copy-done.3 = f32[256,256]{1,0:T(8,128)S(1)} copy-done((f32[256,256]{1,0:T(8,128)S(1)}, f32[256,256]{1,0:T(8,128)}, u32[]{:S(2)}) %copy-start.3) | copy-done | bytes 262168
  4.9 0.0 copy-start.4
  4.9 0.7 %copy-done.4 = s32[16]{0:T(128)S(1)} copy-done((s32[16]{0:T(128)S(1)}, s32[16]{0:T(128)}, u32[]{:S(2)}) %copy-start.4) | copy-done | bytes 88
  5.6 0.0 copy-start.5
  5.6 0.7 %copy-done.5 = f32[4]{0:T(128)S(1)} copy-done((f32[4]{0:T(128)S(1)}, f32[4]{0:T(128)}, u32[]{:S(2)}) %copy-start.5) | copy-done | bytes 40
  6.2 50.5 %combine.1 = f32[1,1,512,256]{3,2,1,0:T(8,128)S(1)} custom-call(s32[16,3]{1,0:T(8,128)S(1)} %copy.9.levels, s32[16]{0:T(128)S(1)} %copy-done.4, f32[4]{0:T(128)S(1)} %copy-done.5, f32[1,1,512,256]{3,2,1,0:T(8,128)S(1)} %copy-done.1, f32[4,256,256]{2,1,0:T(8,128)S(1)} %copy-done, f32[256,256]{1,0:T(8,128)S(1)} %copy-done.3, ...), custom_call_target="tpu_custom_call" | custom-call | tf_op jit(solution)/shard_map/combine/pallas_call | solution.py:461
  56.7 0.8 %copy.11 = f32[1,1,512,256]{3,2,1,0:T(8,128)} copy(f32[1,1,512,256]{3,2,1,0:T(8,128)S(1)} %combine.1) | data formatting | bytes 1048576
Async XLA Ops:
  0.8 1.2 %copy-start = (f32[4,256,256]{2,1,0:T(8,128)S(1)}, f32[4,256,256]{2,1,0:T(8,128)}, u32[]{:S(2)}) copy-start(f32[4,256,256]{2,1,0:T(8,128)} %constant.8.clone.stiff_hbm) | copy-start | bytes 3145732
  2.0 1.0 %copy-start.1 = (f32[1,1,512,256]{3,2,1,0:T(8,128)S(1)}, f32[1,1,512,256]{3,2,1,0:T(8,128)}, u32[]{:S(2)}) copy-start(f32[1,1,512,256]{3,2,1,0:T(8,128)} %x_hbm.1) | copy-start | bytes 1572868
  3.0 0.9 %copy-start.2 = (bf16[2,256,256]{2,1,0:T(8,128)(2,1)S(1)}, bf16[2,256,256]{2,1,0:T(8,128)(2,1)}, u32[]{:S(2)}) copy-start(bf16[2,256,256]{2,1,0:T(8,128)(2,1)} %constant.10.clone.trace_hbm) | copy-start | bytes 786436
  4.0 0.9 %copy-start.3 = (f32[256,256]{1,0:T(8,128)S(1)}, f32[256,256]{1,0:T(8,128)}, u32[]{:S(2)}) copy-start(f32[256,256]{1,0:T(8,128)} %constant.9.clone.lift_hbm) | copy-start | bytes 786436
  4.9 0.7 %copy-start.4 = (s32[16]{0:T(128)S(1)}, s32[16]{0:T(128)}, u32[]{:S(2)}) copy-start(s32[16]{0:T(128)} %coefs.1) | copy-start | bytes 196
  5.6 0.7 %copy-start.5 = (f32[4]{0:T(128)S(1)}, f32[4]{0:T(128)}, u32[]{:S(2)}) copy-start(f32[4]{0:T(128)} %velocity.1) | copy-start | bytes 52
where the time goes:
time: 57.8 us; the launch traced here: 57.5 us
  Pallas kernels  50.5 us (87%)
  local copies, waits for them, and re-layouts  7.03 us (12%)
    pallas_call x1, Pallas kernels, on_device(): pl.pallas_call(functools.partial(kernel, comps, shards), out_shape=jax.Sh...  50.5 us
    unnamed x14, local copies, waits for them, and re-layouts  7.03 us

commit v1 on v0

v1 whole, which is shorter than its diff:
```python
import functools

import jax
import jax.numpy as jnp
import ml_dtypes
import numpy as np
from jax import lax
from jax.experimental import pallas as pl
from jax.experimental.pallas import tpu as pltpu
from jax.sharding import PartitionSpec as P

COEF = 256
BASE = 2
RISE = 3
GRID = 512
LOW = 2**RISE
PLACES = (2**BASE) ** 3
KINDS = (RISE + 1) * (RISE + 2) // 2
BF16 = jnp.bfloat16
F32 = jnp.float32
MESH = pl.DeviceIdType.MESH

courant = 0.1
VMEM_LIMIT = 62 * 2**20
ORDER = (8, 4, 12, 5, 11, 3, 13, 6, 10, 2, 14, 7, 9, 1, 15)
LEFT = [float((-1) ** order * np.sqrt((2 * order + 1) / 2.0)) for order in range(4)]
RIGHT_LEFT = float(sum((-1) ** order * (2 * order + 1) / 2.0 for order in range(4)))


def legendre(order, points):
    values = np.asarray(points) * 1.0
    if order == 0:
        poly = values * 0.0 + 1.0
    elif order == 1:
        poly = values
    elif order == 2:
        poly = (3.0 * values * values - 1.0) / 2.0
    else:
        poly = (5.0 * values * values * values - 3.0 * values) / 2.0
    return np.sqrt((2 * order + 1) / 2.0) * poly


def line_tables():
    nodes = np.array(
        [-0.8611363115940526, -0.3399810435848563, 0.3399810435848563, 0.8611363115940526]
    )
    weights = np.array(
        [0.3478548451374538, 0.6521451548625461, 0.6521451548625461, 0.3478548451374538]
    )
    stiff = np.zeros((4, 4))
    coarse = np.zeros((4, 8))
    for row in range(4):
        for column in range(4):
            if column < row and (row + column) % 2 == 1:
                stiff[row, column] = np.sqrt((2.0 * row + 1.0) * (2.0 * column + 1.0))
            coarse[row, column] = np.sum(
                weights * legendre(row, (nodes - 1.0) / 2.0) * legendre(column, nodes)
            ) / np.sqrt(2.0)
            coarse[row, column + 4] = np.sum(
                weights * legendre(row, (nodes + 1.0) / 2.0) * legendre(column, nodes)
            ) / np.sqrt(2.0)
    right = np.array([float(legendre(order, 1.0)) for order in range(4)])
    left = np.array([float(legendre(order, -1.0)) for order in range(4)])
    rows = [coarse[index] for index in range(4)]
    for index in range(4, 8):
        vector = np.eye(8)[index]
        for other in rows:
            vector = vector - np.dot(other, vector) * other
        rows.append(vector / np.sqrt(np.sum(vector * vector)))
    return (stiff - np.outer(right, right), right, left, np.array(rows))


def along(matrix, axis):
    return np.kron(np.eye(4**axis), np.kron(matrix, np.eye(4 ** (3 - axis))))


def split_table(table):
    hi = table.astype(ml_dtypes.bfloat16)
    lo = (table - hi.astype(np.float64)).astype(ml_dtypes.bfloat16)
    return np.stack([hi, lo], axis=-3)


def line_hierarchy(filters, rise):
    cells = 2**rise
    whole = np.eye(cells * 4).reshape(cells, 4, cells * 4)
    for level_step in range(rise):
        for first in range(0, cells, 2 ** (level_step + 1)):
            second = first + 2**level_step
            pair = np.concatenate([whole[first], whole[second]], axis=0)
            mixed = filters @ pair
            whole[first], whole[second] = mixed[:4], mixed[4:]
    ordered = np.zeros_like(whole)
    for low in range(cells):
        digit = 0
        if low > 0:
            zeros = (low & -low).bit_length() - 1
            height = rise - zeros
            digit = 2 ** (height - 1) + (low >> (zeros + 1))
        ordered[digit] = whole[low]
    return ordered.reshape(cells, 4, cells, 4)


def compositions():
    return [(a, b, RISE - a - b) for a in range(RISE + 1) for b in range(RISE + 1 - a)]


@functools.lru_cache(None)
def tables():
    interior, right, left, filters = line_tables()
    stiff = np.stack([along(interior, axis).T for axis in range(4)]).astype(np.float32)
    lift = np.concatenate([along(left[:, None], axis).T for axis in range(4)]).astype(np.float32)
    trace = np.concatenate([along(right[None, :], axis) for axis in range(4)], axis=0).T
    lines = [line_hierarchy(filters, rise) for rise in range(RISE + 1)]
    hier = []
    for one, two, three in compositions():
        whole = np.einsum("aqlp,brms,cuno->qruabclmnpso", lines[one], lines[two], lines[three])
        hier.append(whole.reshape(GRID, GRID))
    hi, lo = split_table(trace)
    return stiff, lift, np.concatenate([hi, hi, lo]), split_table(np.stack(hier))


def split(values):
    hi = values.astype(BF16)
    return hi, (values - hi.astype(F32)).astype(BF16)


def dot(one, two):
    return jnp.dot(one, two, preferred_element_type=F32)


def dot_nt(one, two):
    return lax.dot_general(one, two, (((1,), (1,)), ((), ())), preferred_element_type=F32)


def triple(hi, lo):
    return jnp.concatenate([hi, lo, hi], axis=1)


def kernel(
    comps,
    shards,
    levels_hbm,
    coefs_hbm,
    velocity_hbm,
    x_hbm,
    stiff_hbm,
    lift_hbm,
    trace_hbm,
    hier_hbm,
    out_ref,
    levels,
    coefs,
    velocity,
    x_v,
    stiff_v,
    lift_v,
    trace_v,
    hier_v,
    onehot,
    match,
    wide,
    lifts,
    field,
    traces1,
    traces2,
    shifted,
    section,
    edge_out,
    edge_in,
    rows,
    sent,
    got,
    back,
    home,
    local_sem,
    edge_send,
    edge_recv,
    there_send,
    there_recv,
    back_send,
    back_recv,
):
    me = lax.axis_index("comp")
    spot = lax.axis_index("shard")
    ahead = lax.rem(spot + 1, shards)
    behind = lax.rem(spot + shards - 1, shards)

    def fetch(source, target, index):
        copy = pltpu.make_async_copy(source, target, local_sem.at[index])
        copy.start()
        return copy

    levels_copy = fetch(levels_hbm, levels, 0)
    x_copy = fetch(x_hbm.at[0, 0], x_v, 1)
    velocity_copy = fetch(velocity_hbm, velocity, 2)
    trace_copy = fetch(trace_hbm, trace_v, 3)
    stiff_copy = fetch(stiff_hbm, stiff_v, 4)
    lift_copy = fetch(lift_hbm, lift_v, 5)
    coefs_copy = fetch(coefs_hbm, coefs, 6)
    hier_copy = fetch(hier_hbm, hier_v, 7)

    barrier = pltpu.get_barrier_semaphore()
    for step in range(1, comps):
        pl.semaphore_signal(
            barrier, inc=1, device_id={"comp": lax.rem(me + step, comps)}, device_id_type=MESH
        )
    pl.semaphore_signal(barrier, inc=1, device_id={"shard": ahead}, device_id_type=MESH)
    pl.semaphore_signal(barrier, inc=1, device_id={"shard": behind}, device_id_type=MESH)

    levels_copy.wait()

    def rise_of(comp, axis):
        return jnp.clip(levels[axis, comp] - BASE, 0, RISE)

    rise1 = rise_of(me, 0)
    rise2 = rise_of(me, 1)
    rise3 = rise_of(me, 2)
    kind = jnp.clip(lax.shift_right_logical(rise1 * (9 - rise1), 1) + rise2, 0, KINDS - 1)
    one = jnp.int32(1)

    def low_digits(low):
        low3 = low & (lax.shift_left(one, rise3) - 1)
        low2 = lax.shift_right_logical(low, rise3) & (lax.shift_left(one, rise2) - 1)
        low1 = lax.shift_right_logical(low, rise2 + rise3)
        return low1, low2, low3

    def cell_of(digit1, digit2, digit3):
        return (
            lax.shift_left(digit1, rise2 + rise3 + 2 * BASE)
            + lax.shift_left(digit2, rise3 + BASE)
            + digit3
        )

    offsets = [cell_of(*low_digits(jnp.int32(low))) for low in range(LOW)]

    def place_cell(place):
        return cell_of(
            lax.shift_left(lax.shift_right_logical(place, 4) & 3, jnp.full(place.shape, rise1)),
            lax.shift_left(lax.shift_right_logical(place, 2) & 3, jnp.full(place.shape, rise2)),
            lax.shift_left(place & 3, jnp.full(place.shape, rise3)),
        )

    place_row = lax.broadcasted_iota(jnp.int32, (PLACES, 128), 0)
    lanes = lax.broadcasted_iota(jnp.int32, (PLACES, 128), 1)
    left_half = lanes < 64
    place_rows = place_cell(place_row)
    for low in range(LOW):
        for part in range(GRID // 128):
            hit = (place_rows + offsets[low]) == (lanes + 128 * part)
            onehot[low * PLACES : (low + 1) * PLACES, 128 * part : 128 * (part + 1)] = jnp.where(
                hit, 1.0, 0.0
            ).astype(BF16)

    x_copy.wait()
    hi, lo = split(x_v[...])
    new_hi, new_lo = dot(onehot[...], hi), dot(onehot[...], lo)
    field[...] = new_hi + new_lo
    thrice = triple(new_hi.astype(BF16), new_lo.astype(BF16))

    def halves(one, two):
        return jnp.where(left_half, one, two)

    def swap(values):
        return pltpu.roll(values, 64, 1)

    def block_of(low):
        return slice(low * PLACES, (low + 1) * PLACES)

    def pack(values, low):
        return halves(values[block_of(low), :], swap(values[block_of(low + LOW // 2), :]))

    def send_edge(stage):
        copy = pltpu.make_async_remote_copy(
            src_ref=edge_out.at[stage],
            dst_ref=edge_in.at[stage],
            send_sem=edge_send.at[stage],
            recv_sem=edge_recv.at[stage],
            device_id={"shard": ahead},
            device_id_type=MESH,
        )
        copy.start()
        return copy

    trace_copy.wait()
    trace = dot(thrice, trace_v[...])
    for low in range(LOW // 2):
        edge_out[0, low] = pack(trace[:, :128], low)
    pl.semaphore_wait(barrier, comps + 1)
    edge_copy = send_edge(0)

    velocity_copy.wait()
    reach = None
    for comp in range(comps):
        total = velocity[0] * (1.0 * shards)
        for axis in range(3):
            size = lax.shift_left(one, levels[axis, comp]).astype(F32)
            total = total + velocity[axis + 1] * size
        reach = total if reach is None else jnp.maximum(reach, total)
    step_size = jnp.full((1, COEF), courant, F32) / jnp.full((1, COEF), reach, F32)
    sizes = [jnp.float32(shards)] + [
        lax.shift_left(one, levels[axis, me]).astype(F32) for axis in range(3)
    ]
    scales = [step_size * (2.0 * velocity[axis] * sizes[axis]) for axis in range(4)]
    stiff_copy.wait()
    volume = scales[0] * stiff_v[0]
    for axis in range(1, 4):
        volume = volume + scales[axis] * stiff_v[axis]
    hi, lo = split(volume)
    wide[:COEF], wide[COEF : 2 * COEF], wide[2 * COEF :] = hi, hi, lo
    lift_copy.wait()
    for part in range(3):
        lifts[part * COEF : part * COEF + 64, :] = jnp.zeros((64, COEF), BF16)
    for axis in range(1, 4):
        hi, lo = split(scales[axis] * lift_v[64 * axis : 64 * (axis + 1), :])
        for part, piece in enumerate((hi, hi, lo)):
            start = part * COEF + 64 * axis
            lifts[start : start + 64, :] = piece
    lift_first = [
        scales[0][:, :128] * jnp.where(left_half[:1], LEFT[2 * group], LEFT[2 * group + 1])
        for group in range(2)
    ]
    edge_factor = scales[0][:, :128] * RIGHT_LEFT

    def behind_of(low, axis):
        digits = list(low_digits(jnp.int32(low)))
        rise = (rise1, rise2, rise3)[axis]
        first = digits[axis] == 0
        digits[axis] = (digits[axis] + lax.shift_left(one, rise) - 1) & (
            lax.shift_left(one, rise) - 1
        )
        spot = (
            lax.shift_left(digits[0], rise2 + rise3) + lax.shift_left(digits[1], rise3) + digits[2]
        )
        return spot & (LOW - 1), first

    sources = []
    for low in range(LOW):
        spot1, first1 = behind_of(low, 0)
        spot2, first2 = behind_of(low, 1)
        spot3, first3 = behind_of(low, 2)
        sources.append(
            (
                spot1 + jnp.where(first1, LOW, 0),
                spot2 + jnp.where(first2, LOW, 0),
                spot3 + jnp.where(first3, 2 * LOW, 0),
            )
        )

    def inner_slope(thrice, trace):
        for low in range(LOW):
            now = trace[block_of(low), :128]
            traces1[low] = now
            traces1[LOW + low] = pltpu.roll(now, 16, 0)
            now = trace[block_of(low), 128:]
            traces2[low] = now
            traces2[LOW + low] = jnp.where(
                (place_row & 15) < 4, pltpu.roll(now, PLACES - 12, 0), pltpu.roll(now, 4, 0)
            )
            traces2[2 * LOW + low] = jnp.where(
                (place_row & 3) < 1, pltpu.roll(now, PLACES - 3, 0), pltpu.roll(now, 1, 0)
            )
        inner = dot(thrice, wide[...])
        for low in range(LOW):
            from1, from2, from3 = sources[low]
            shifted[block_of(low), :128] = traces1[from1]
            shifted[block_of(low), 128:] = halves(traces2[from2], traces2[from3])
        return inner + dot(triple(*split(shifted[...])), lifts[...])

    def add_edge(stage, factor):
        for low in range(LOW // 2):
            edge = edge_in[stage, low]
            turned = swap(edge)
            for place, both in (
                (low, halves(edge, turned)),
                (low + LOW // 2, halves(turned, edge)),
            ):
                for group in range(2):
                    columns = slice(128 * group, 128 * (group + 1))
                    section[block_of(place), columns] += (factor * lift_first[group]) * both

    section[...] = field[...] + inner_slope(thrice, trace)
    trace = dot(triple(*split(section[...])), trace_v[:, :128])
    for low in range(LOW // 2):
        edge_out[1, low] = pack(trace, low)
    edge_copy.wait()
    for low in range(LOW // 2):
        edge_out[1, low] += edge_factor * edge_in[0, low]
    edge_copy = send_edge(1)
    add_edge(0, 1.0)

    thrice = triple(*split(section[...]))
    trace = dot(thrice, trace_v[...])
    section[...] = 0.5 * field[...] + 0.5 * (section[...] + inner_slope(thrice, trace))
    edge_copy.wait()
    add_edge(1, 0.5)

    def exchange(source, target, half, send_sem, recv_sem):
        copies = []
        for step in ORDER:
            other = lax.rem(me + step, comps)
            copy = pltpu.make_async_remote_copy(
                src_ref=source.at[half, other],
                dst_ref=target.at[half, me],
                send_sem=send_sem.at[half, step],
                recv_sem=recv_sem.at[half, step],
                device_id={"comp": other},
                device_id_type=MESH,
            )
            copy.start()
            copies.append(copy)
        target[half, me] = source[half, me]
        return copies

    there = []
    for half in range(2):
        columns = slice(128 * half, 128 * (half + 1))
        for pair in range(LOW // 2):
            even = section[block_of(2 * pair), columns]
            odd = section[block_of(2 * pair + 1), columns]
            into = slice(128 * pair, 128 * (pair + 1))
            hi, lo = split(jnp.concatenate([halves(even, swap(odd)), halves(swap(even), odd)]))
            rows[half, :128, into] = hi
            rows[half, 128:, into] = lo
        if half == 0:
            hier_copy.wait()
            h_hi, h_lo = hier_v[kind, 0], hier_v[kind, 1]
        both = dot_nt(h_hi, rows[half])
        whole = both[:, :128] + both[:, 128:] + dot_nt(h_lo, rows[half, :128])
        sent[half] = whole.reshape(sent.shape[1:])
        there.append(exchange(sent, got, half, there_send, there_recv))

    coefs_copy.wait()

    def code_of(digits, comp):
        up2 = rise_of(comp, 1)
        up3 = rise_of(comp, 2)
        digit3 = digits & (lax.shift_left(one, up3) - 1)
        digit2 = lax.shift_right_logical(digits, jnp.full(digits.shape, up3)) & (
            lax.shift_left(one, up2) - 1
        )
        digit1 = lax.shift_right_logical(digits, jnp.full(digits.shape, up2 + up3))
        return digit1 * 64 + digit2 * 8 + digit3

    piece_row = lax.broadcasted_iota(jnp.int32, (8, 128), 0)
    piece_lane = lax.broadcasted_iota(jnp.int32, (8, 128), 1)
    lane_code = jnp.zeros((8, 128), jnp.int32)
    lane_coef = jnp.zeros((8, 128), F32)
    for comp in range(comps):
        own = lax.shift_right_logical(piece_lane, 3) == comp
        lane_code = jnp.where(own, code_of(piece_lane & 7, comp), lane_code)
        lane_coef = jnp.where(own, jnp.full((8, 128), coefs[comp].astype(F32)), lane_coef)
    for comp in range(0, comps, 2):
        block = [
            jnp.where(code_of(piece_row, here) == lane_code, lane_coef, 0.0)
            for here in (comp, comp + 1)
        ]
        match[8 * comp : 8 * comp + 16, :] = jnp.concatenate(block, axis=0).astype(BF16)

    cell_rows = lax.broadcasted_iota(jnp.int32, (GRID, 128), 0)
    lane_place = place_cell(piece_lane & (PLACES - 1))
    for part in range(GRID // 128):
        lane_cell = lane_place + jnp.where(
            piece_lane < 64, offsets[2 * part], offsets[2 * part + 1]
        )
        onehot[:, 128 * part : 128 * (part + 1)] = jnp.where(
            cell_rows == lane_cell[0:1, :], 1.0, 0.0
        ).astype(BF16)

    homeward = []
    for half in range(2):
        for copy in there[half]:
            copy.wait()
        for quarter in range(4):
            part = slice(8 * quarter, 8 * (quarter + 1))
            hi, lo = split(got[half, :, part, :].reshape(8 * comps, 128))
            both = dot(match[...], jnp.concatenate([hi, lo], axis=1))
            back[half, :, part, :] = (both[:, :128] + both[:, 128:]).reshape(comps, 8, 128)
        homeward.append(exchange(back, home, half, back_send, back_recv))

    for half in range(2):
        for copy in homeward[half]:
            copy.wait()
        hi, lo = split(home[half].reshape(GRID, 128).T)
        both = dot(jnp.concatenate([hi, lo]), h_hi)
        plain = both[:128] + both[128:] + dot(hi, h_lo)
        for pair in range(LOW // 2):
            into = slice(128 * pair, 128 * (pair + 1))
            upper, lower = plain[:64, into], plain[64:, into]
            section[block_of(2 * pair), :128] = halves(upper, swap(lower))
            section[block_of(2 * pair + 1), :128] = halves(swap(upper), lower)
        both = dot(onehot[...], jnp.concatenate(split(section[:, :128]), axis=1))
        out_ref[0, 0, :, 128 * half : 128 * (half + 1)] = both[:, :128] + both[:, 128:]


def on_device(modal_coefs, comp_levels, comp_coefs, velocity):
    comps = lax.axis_size("comp")
    shards = lax.axis_size("shard")
    stiff, lift, trace, hier = tables()
    anywhere = pl.BlockSpec(memory_space=pl.ANY)
    dma = pltpu.SemaphoreType.DMA
    exchanged = pltpu.VMEM((2, comps, GRID // comps, 128), F32)
    return pl.pallas_call(
        functools.partial(kernel, comps, shards),
        out_shape=jax.ShapeDtypeStruct(modal_coefs.shape, F32),
        in_specs=[anywhere] * 8,
        out_specs=pl.BlockSpec(memory_space=pltpu.VMEM),
        scratch_shapes=[
            pltpu.SMEM((3, comps), jnp.int32),
            pltpu.SMEM((comps,), jnp.int32),
            pltpu.SMEM((4,), F32),
            pltpu.VMEM((GRID, COEF), F32),
            pltpu.VMEM(stiff.shape, F32),
            pltpu.VMEM(lift.shape, F32),
            pltpu.VMEM(trace.shape, BF16),
            pltpu.VMEM(hier.shape, BF16),
            pltpu.VMEM((GRID, GRID), BF16),
            pltpu.VMEM((8 * comps, 8 * comps), BF16),
            pltpu.VMEM((3 * COEF, COEF), BF16),
            pltpu.VMEM((3 * COEF, COEF), BF16),
            pltpu.VMEM((GRID, COEF), F32),
            pltpu.VMEM((2 * LOW, PLACES, 128), F32),
            pltpu.VMEM((3 * LOW, PLACES, 128), F32),
            pltpu.VMEM((GRID, COEF), F32),
            pltpu.VMEM((GRID, COEF), F32),
            pltpu.VMEM((2, LOW // 2, PLACES, 128), F32),
            pltpu.VMEM((2, LOW // 2, PLACES, 128), F32),
            pltpu.VMEM((2, 2 * 128, GRID), BF16),
            exchanged,
            exchanged,
            exchanged,
            exchanged,
            dma((8,)),
            dma((2,)),
            dma((2,)),
            dma((2, comps)),
            dma((2, comps)),
            dma((2, comps)),
            dma((2, comps)),
        ],
        compiler_params=pltpu.CompilerParams(
            collective_id=0, has_side_effects=True, vmem_limit_bytes=VMEM_LIMIT
        ),
        name="combine",
    )(
        comp_levels.T,
        comp_coefs,
        velocity,
        modal_coefs,
        jnp.asarray(stiff),
        jnp.asarray(lift),
        jnp.asarray(trace),
        jnp.asarray(hier),
    )


def solution(mesh):
    placed = (P("comp", "shard", None, None), P(), P(), P())
    return jax.shard_map(
        on_device,
        mesh=mesh,
        in_specs=placed,
        out_specs=P("comp", "shard", None, None),
        check_vma=False,
    )
```

time: 57.8 us -> 46.8 us (0.81)
  the two profiles are of different devices: /device:TPU:1 before, /device:TPU:2 now
where the time goes in v1:
time: 46.8 us; the launch traced here: 46.7 us
  Pallas kernels  44.8 us (96%)
  local copies, waits for them, and re-layouts  1.87 us (4%)
    pallas_call x1, Pallas kernels, on_device(): pl.pallas_call(functools.partial(kernel, comps, shards), out_shape=jax.Sh...  44.8 us
    unnamed x1, local copies, waits for them, and re-layouts  1.87 us

profile of v1, /device:TPU:2, one launch (start us, length us, event | category | flops | bytes accessed | tf_op | source)
XLA Modules:
  0.0 46.7 jit_solution(6637763801712186553)
XLA Ops:
  0.0 44.8 %combine.1 = f32[1,1,512,256]{3,2,1,0:T(8,128)} custom-call(s32[3,16]{1,0:T(4,128)} %bitcast.1, s32[16]{0:T(128)} %coefs_hbm.1, f32[4]{0:T(128)} %velocity_hbm.1, f32[1,1,512,256]{3,2,1,0:T(8,128)} %x_hbm.1, f32[4,256,256]{2,1,0:T(8,128)} %constant.8.clone.stiff_hbm, f32[256,256]{1,0:T(8,128)} %constant.9.clone.lift_hbm, ...), custom_call_target="tpu_custom_call" | custom-call | tf_op jit(solution)/shard_map/combine/pallas_call | solution.py:502
  44.8 1.9 %copy.10 = f32[1,1,512,256]{3,2,1,0:T(8,128)} copy(f32[1,1,512,256]{3,2,1,0:T(8,128)} %combine.1) | data formatting | bytes 1048576

commit v2 on v1

--- a/solution.py
+++ b/solution.py
@@ -72,6 +72,12 @@
 
 def along(matrix, axis):
     return np.kron(np.eye(4**axis), np.kron(matrix, np.eye(4 ** (3 - axis))))
+
+
+def first_basis():
+    interior, _, left, _ = line_tables()
+    turned, _ = np.linalg.qr(np.stack([left, interior @ left], axis=1), mode="complete")
+    return np.concatenate([turned[:, 2:], turned[:, :2]], axis=1).T
 
 
 def split_table(table):
@@ -165,6 +171,7 @@
     traces2,
     shifted,
     section,
+    inside,
     edge_out,
     edge_in,
     rows,
@@ -378,21 +385,10 @@
                     columns = slice(128 * group, 128 * (group + 1))
                     section[block_of(place), columns] += (factor * lift_first[group]) * both
 
-    section[...] = field[...] + inner_slope(thrice, trace)
-    trace = dot(triple(*split(section[...])), trace_v[:, :128])
-    for low in range(LOW // 2):
-        edge_out[1, low] = pack(trace, low)
-    edge_copy.wait()
-    for low in range(LOW // 2):
-        edge_out[1, low] += edge_factor * edge_in[0, low]
-    edge_copy = send_edge(1)
-    add_edge(0, 1.0)
-
-    thrice = triple(*split(section[...]))
-    trace = dot(thrice, trace_v[...])
-    section[...] = 0.5 * field[...] + 0.5 * (section[...] + inner_slope(thrice, trace))
-    edge_copy.wait()
-    add_edge(1, 0.5)
+    def advance(trace, thrice):
+        return 0.5 * field[...] + 0.5 * (section[...] + inner_slope(thrice, trace))
+
+    basis = first_basis()
 
     def exchange(source, target, half, send_sem, recv_sem):
         copies = []
@@ -411,23 +407,49 @@
         target[half, me] = source[half, me]
         return copies
 
-    there = []
-    for half in range(2):
-        columns = slice(128 * half, 128 * (half + 1))
+    def to_owners(half):
         for pair in range(LOW // 2):
-            even = section[block_of(2 * pair), columns]
-            odd = section[block_of(2 * pair + 1), columns]
+            blocks = []
+            for group in range(2):
+                columns = slice(128 * group, 128 * (group + 1))
+                even = section[block_of(2 * pair), columns]
+                odd = section[block_of(2 * pair + 1), columns]
+                blocks += [halves(even, swap(odd)), halves(swap(even), odd)]
+            turned = [
+                sum(float(basis[row, first]) * blocks[first] for first in range(4))
+                for row in (2 * half, 2 * half + 1)
+            ]
             into = slice(128 * pair, 128 * (pair + 1))
-            hi, lo = split(jnp.concatenate([halves(even, swap(odd)), halves(swap(even), odd)]))
+            hi, lo = split(jnp.concatenate(turned))
             rows[half, :128, into] = hi
             rows[half, 128:, into] = lo
-        if half == 0:
-            hier_copy.wait()
-            h_hi, h_lo = hier_v[kind, 0], hier_v[kind, 1]
         both = dot_nt(h_hi, rows[half])
         whole = both[:, :128] + both[:, 128:] + dot_nt(h_lo, rows[half, :128])
         sent[half] = whole.reshape(sent.shape[1:])
-        there.append(exchange(sent, got, half, there_send, there_recv))
+        return exchange(sent, got, half, there_send, there_recv)
+
+    section[...] = field[...] + inner_slope(thrice, trace)
+    inside[...] = section[...]
+    thrice = triple(*split(section[...]))
+    trace = dot(thrice, trace_v[...])
+    for low in range(LOW // 2):
+        edge_out[1, low] = pack(trace[:, :128], low)
+    section[...] = advance(trace, thrice)
+    edge_copy.wait()
+    for low in range(LOW // 2):
+        edge_out[1, low] += edge_factor * edge_in[0, low]
+    edge_copy = send_edge(1)
+    hier_copy.wait()
+    h_hi, h_lo = hier_v[kind, 0], hier_v[kind, 1]
+    there = [to_owners(0)]
+
+    section[...] = inside[...]
+    add_edge(0, 1.0)
+    thrice = triple(*split(section[...]))
+    section[...] = advance(dot(thrice, trace_v[...]), thrice)
+    edge_copy.wait()
+    add_edge(1, 0.5)
+    there.append(to_owners(1))
 
     coefs_copy.wait()
 
@@ -489,7 +511,20 @@
             section[block_of(2 * pair), :128] = halves(upper, swap(lower))
             section[block_of(2 * pair + 1), :128] = halves(swap(upper), lower)
         both = dot(onehot[...], jnp.concatenate(split(section[:, :128]), axis=1))
-        out_ref[0, 0, :, 128 * half : 128 * (half + 1)] = both[:, :128] + both[:, 128:]
+        turned = both[:, :128] + both[:, 128:]
+        swapped = swap(turned)
+        for group in range(2):
+            near = [float(basis[2 * half + k, 2 * group + k]) for k in range(2)]
+            far = [float(basis[2 * half + 1 - k, 2 * group + k]) for k in range(2)]
+            part = (
+                jnp.where(left_half[:1], near[0], near[1]) * turned
+                + jnp.where(left_half[:1], far[0], far[1]) * swapped
+            )
+            columns = slice(128 * group, 128 * (group + 1))
+            if half == 0:
+                out_ref[0, 0, :, columns] = part
+            else:
+                out_ref[0, 0, :, columns] += part
 
 
 def on_device(modal_coefs, comp_levels, comp_coefs, velocity):
@@ -520,6 +555,7 @@
             pltpu.VMEM((GRID, COEF), F32),
             pltpu.VMEM((2 * LOW, PLACES, 128), F32),
             pltpu.VMEM((3 * LOW, PLACES, 128), F32),
+            pltpu.VMEM((GRID, COEF), F32),
             pltpu.VMEM((GRID, COEF), F32),
             pltpu.VMEM((GRID, COEF), F32),
             pltpu.VMEM((2, LOW // 2, PLACES, 128), F32),

time: 46.8 us -> 43.2 us (0.923)
  Pallas kernels: 44.8 us -> 41.2 us
    pallas_call x1, Pallas kernels: 44.8 us -> 41.2 us  [on_device(): pl.pallas_call(functools.partial(kernel, comps, shards), out_shape=jax.Sh...]
where the time goes in v2:
time: 43.2 us; the launch traced here: 43.1 us
  Pallas kernels  41.2 us (95%)
  local copies, waits for them, and re-layouts  1.87 us (4%)
    pallas_call x1, Pallas kernels, on_device(): pl.pallas_call(functools.partial(kernel, comps, shards), out_shape=jax.Sh...  41.2 us
    unnamed x1, local copies, waits for them, and re-layouts  1.87 us

profile of v2, /device:TPU:2, one launch (start us, length us, event | category | flops | bytes accessed | tf_op | source)
XLA Modules:
  0.0 43.1 jit_solution(8600754097314037478)
XLA Ops:
  0.0 41.2 %combine.1 = f32[1,1,512,256]{3,2,1,0:T(8,128)} custom-call(s32[3,16]{1,0:T(4,128)} %bitcast.1, s32[16]{0:T(128)} %coefs_hbm.1, f32[4]{0:T(128)} %velocity_hbm.1, f32[1,1,512,256]{3,2,1,0:T(8,128)} %x_hbm.1, f32[4,256,256]{2,1,0:T(8,128)} %constant.8.clone.stiff_hbm, f32[256,256]{1,0:T(8,128)} %constant.9.clone.lift_hbm, ...), custom_call_target="tpu_custom_call" | custom-call | tf_op jit(solution)/shard_map/combine/pallas_call | solution.py:537
  41.2 1.9 %copy.10 = f32[1,1,512,256]{3,2,1,0:T(8,128)} copy(f32[1,1,512,256]{3,2,1,0:T(8,128)} %combine.1) | data formatting | bytes 1048576

commit v3 on v2

--- a/solution.py
+++ b/solution.py
@@ -23,7 +23,6 @@
 courant = 0.1
 VMEM_LIMIT = 62 * 2**20
 ORDER = (8, 4, 12, 5, 11, 3, 13, 6, 10, 2, 14, 7, 9, 1, 15)
-LEFT = [float((-1) ** order * np.sqrt((2 * order + 1) / 2.0)) for order in range(4)]
 RIGHT_LEFT = float(sum((-1) ** order * (2 * order + 1) / 2.0 for order in range(4)))
 
 
@@ -71,7 +70,11 @@
 
 
 def along(matrix, axis):
-    return np.kron(np.eye(4**axis), np.kron(matrix, np.eye(4 ** (3 - axis))))
+    return np.kron(np.eye(4**axis), np.kron(matrix, np.eye(4 ** (2 - axis))))
+
+
+def twice(matrix):
+    return np.kron(np.eye(2), matrix)
 
 
 def first_basis():
@@ -113,16 +116,20 @@
 @functools.lru_cache(None)
 def tables():
     interior, right, left, filters = line_tables()
-    stiff = np.stack([along(interior, axis).T for axis in range(4)]).astype(np.float32)
-    lift = np.concatenate([along(left[:, None], axis).T for axis in range(4)]).astype(np.float32)
-    trace = np.concatenate([along(right[None, :], axis) for axis in range(4)], axis=0).T
+    stiff = np.stack([twice(along(interior, axis).T) for axis in range(3)]).astype(np.float32)
+    lift = np.zeros((128, 128), np.float32)
+    trace = np.zeros((128, 128))
+    for axis in range(3):
+        lift[32 * axis : 32 * (axis + 1)] = twice(along(left[:, None], axis).T)
+        trace[:, 32 * axis : 32 * (axis + 1)] = twice(along(right[None, :], axis).T)
     lines = [line_hierarchy(filters, rise) for rise in range(RISE + 1)]
     hier = []
     for one, two, three in compositions():
         whole = np.einsum("aqlp,brms,cuno->qruabclmnpso", lines[one], lines[two], lines[three])
         hier.append(whole.reshape(GRID, GRID))
     hi, lo = split_table(trace)
-    return stiff, lift, np.concatenate([hi, hi, lo]), split_table(np.stack(hier))
+    trace = np.block([[hi, lo], [hi, np.zeros_like(lo)]])
+    return stiff, lift, trace, split_table(np.stack(hier))
 
 
 def split(values):
@@ -138,8 +145,16 @@
     return lax.dot_general(one, two, (((1,), (1,)), ((), ())), preferred_element_type=F32)
 
 
-def triple(hi, lo):
-    return jnp.concatenate([hi, lo, hi], axis=1)
+def fold(values):
+    return values[:, :128] + values[:, 128:]
+
+
+def square(matrix):
+    hi, lo = split(matrix)
+    zero = jnp.zeros_like(lo)
+    return jnp.concatenate(
+        [jnp.concatenate([hi, lo], axis=1), jnp.concatenate([hi, zero], axis=1)], axis=0
+    )
 
 
 def kernel(
@@ -167,11 +182,10 @@
     wide,
     lifts,
     field,
-    traces1,
-    traces2,
+    other,
+    traces,
     shifted,
-    section,
-    inside,
+    plane,
     edge_out,
     edge_in,
     rows,
@@ -258,26 +272,44 @@
                 hit, 1.0, 0.0
             ).astype(BF16)
 
+    def halves(one, two):
+        return jnp.where(left_half, one, two)
+
+    def swap(values):
+        return pltpu.roll(values, 64, 1)
+
+    def block_of(low):
+        return slice(low * PLACES, (low + 1) * PLACES)
+
+    def blocks(values):
+        return [values[block_of(low), :] for low in range(LOW)]
+
     x_copy.wait()
     hi, lo = split(x_v[...])
-    new_hi, new_lo = dot(onehot[...], hi), dot(onehot[...], lo)
-    field[...] = new_hi + new_lo
-    thrice = triple(new_hi.astype(BF16), new_lo.astype(BF16))
-
-    def halves(one, two):
-        return jnp.where(left_half, one, two)
-
-    def swap(values):
-        return pltpu.roll(values, 64, 1)
-
-    def block_of(low):
-        return slice(low * PLACES, (low + 1) * PLACES)
-
-    def pack(values, low):
-        return halves(values[block_of(low), :], swap(values[block_of(low + LOW // 2), :]))
-
-    def send_edge(stage):
-        copy = pltpu.make_async_remote_copy(
+    now = dot(onehot[...], hi) + dot(onehot[...], lo)
+    field[...] = now
+    other[:, :128] = swap(now[:, :128])
+    other[:, 128:] = swap(now[:, 128:])
+
+    basis = first_basis()
+    interior, right, left, _ = line_tables()
+
+    def pair_of(rows_of):
+        return [
+            jnp.where(left_half[:1], float(rows_of[0][first]), float(rows_of[1][second]))
+            for first, second in ((0, 1), (1, 0), (2, 3), (3, 2))
+        ]
+
+    def mix(factors):
+        return (
+            factors[0] * field[:, :128]
+            + factors[1] * other[:, :128]
+            + factors[2] * field[:, 128:]
+            + factors[3] * other[:, 128:]
+        )
+
+    def edge_copy(stage):
+        return pltpu.make_async_remote_copy(
             src_ref=edge_out.at[stage],
             dst_ref=edge_in.at[stage],
             send_sem=edge_send.at[stage],
@@ -285,15 +317,16 @@
             device_id={"shard": ahead},
             device_id_type=MESH,
         )
-        copy.start()
-        return copy
-
-    trace_copy.wait()
-    trace = dot(thrice, trace_v[...])
-    for low in range(LOW // 2):
-        edge_out[0, low] = pack(trace[:, :128], low)
+
+    def pack(stage, values):
+        parts = blocks(values)
+        for low in range(LOW // 2):
+            edge_out[stage, low] = halves(parts[low], parts[low + LOW // 2])
+
+    pack(0, mix(pair_of([right, right])))
     pl.semaphore_wait(barrier, comps + 1)
-    edge_copy = send_edge(0)
+    first_edge, second_edge = edge_copy(0), edge_copy(1)
+    first_edge.start()
 
     velocity_copy.wait()
     reach = None
@@ -303,30 +336,22 @@
             size = lax.shift_left(one, levels[axis, comp]).astype(F32)
             total = total + velocity[axis + 1] * size
         reach = total if reach is None else jnp.maximum(reach, total)
-    step_size = jnp.full((1, COEF), courant, F32) / jnp.full((1, COEF), reach, F32)
+    step_size = jnp.full((1, 128), courant, F32) / jnp.full((1, 128), reach, F32)
     sizes = [jnp.float32(shards)] + [
         lax.shift_left(one, levels[axis, me]).astype(F32) for axis in range(3)
     ]
-    scales = [step_size * (2.0 * velocity[axis] * sizes[axis]) for axis in range(4)]
+    first_scale, *scales = [
+        step_size * (2.0 * velocity[axis] * sizes[axis]) for axis in range(4)
+    ]
     stiff_copy.wait()
-    volume = scales[0] * stiff_v[0]
-    for axis in range(1, 4):
-        volume = volume + scales[axis] * stiff_v[axis]
-    hi, lo = split(volume)
-    wide[:COEF], wide[COEF : 2 * COEF], wide[2 * COEF :] = hi, hi, lo
+    wide[...] = square(
+        scales[0] * stiff_v[0] + scales[1] * stiff_v[1] + scales[2] * stiff_v[2]
+    )
     lift_copy.wait()
-    for part in range(3):
-        lifts[part * COEF : part * COEF + 64, :] = jnp.zeros((64, COEF), BF16)
-    for axis in range(1, 4):
-        hi, lo = split(scales[axis] * lift_v[64 * axis : 64 * (axis + 1), :])
-        for part, piece in enumerate((hi, hi, lo)):
-            start = part * COEF + 64 * axis
-            lifts[start : start + 64, :] = piece
-    lift_first = [
-        scales[0][:, :128] * jnp.where(left_half[:1], LEFT[2 * group], LEFT[2 * group + 1])
-        for group in range(2)
-    ]
-    edge_factor = scales[0][:, :128] * RIGHT_LEFT
+    scale_rows = [jnp.broadcast_to(scale, (32, 128)) for scale in scales]
+    lifts[...] = square(
+        jnp.concatenate([*scale_rows, jnp.zeros((32, 128), F32)], axis=0) * lift_v[...]
+    )
 
     def behind_of(low, axis):
         digits = list(low_digits(jnp.int32(low)))
@@ -338,57 +363,49 @@
         spot = (
             lax.shift_left(digits[0], rise2 + rise3) + lax.shift_left(digits[1], rise3) + digits[2]
         )
-        return spot & (LOW - 1), first
-
-    sources = []
-    for low in range(LOW):
-        spot1, first1 = behind_of(low, 0)
-        spot2, first2 = behind_of(low, 1)
-        spot3, first3 = behind_of(low, 2)
-        sources.append(
-            (
-                spot1 + jnp.where(first1, LOW, 0),
-                spot2 + jnp.where(first2, LOW, 0),
-                spot3 + jnp.where(first3, 2 * LOW, 0),
+        return (spot & (LOW - 1)) + jnp.where(first, LOW, 0)
+
+    sources = [[behind_of(low, axis) for axis in range(3)] for low in range(LOW)]
+
+    def by_axis(one, two, three):
+        return jnp.where(lanes < 32, one, jnp.where(lanes < 64, two, three))
+
+    def others_step(values):
+        pair = jnp.concatenate(split(values), axis=1)
+        for low, now in enumerate(blocks(fold(dot(pair, trace_v[...])))):
+            traces[low] = now
+            traces[LOW + low] = by_axis(
+                pltpu.roll(now, 16, 0),
+                jnp.where(
+                    (place_row & 15) < 4, pltpu.roll(now, PLACES - 12, 0), pltpu.roll(now, 4, 0)
+                ),
+                jnp.where(
+                    (place_row & 3) < 1, pltpu.roll(now, PLACES - 3, 0), pltpu.roll(now, 1, 0)
+                ),
             )
-        )
-
-    def inner_slope(thrice, trace):
+        inner = dot(pair, wide[...])
         for low in range(LOW):
-            now = trace[block_of(low), :128]
-            traces1[low] = now
-            traces1[LOW + low] = pltpu.roll(now, 16, 0)
-            now = trace[block_of(low), 128:]
-            traces2[low] = now
-            traces2[LOW + low] = jnp.where(
-                (place_row & 15) < 4, pltpu.roll(now, PLACES - 12, 0), pltpu.roll(now, 4, 0)
-            )
-            traces2[2 * LOW + low] = jnp.where(
-                (place_row & 3) < 1, pltpu.roll(now, PLACES - 3, 0), pltpu.roll(now, 1, 0)
-            )
-        inner = dot(thrice, wide[...])
-        for low in range(LOW):
-            from1, from2, from3 = sources[low]
-            shifted[block_of(low), :128] = traces1[from1]
-            shifted[block_of(low), 128:] = halves(traces2[from2], traces2[from3])
-        return inner + dot(triple(*split(shifted[...])), lifts[...])
-
-    def add_edge(stage, factor):
-        for low in range(LOW // 2):
-            edge = edge_in[stage, low]
-            turned = swap(edge)
-            for place, both in (
-                (low, halves(edge, turned)),
-                (low + LOW // 2, halves(turned, edge)),
-            ):
-                for group in range(2):
-                    columns = slice(128 * group, 128 * (group + 1))
-                    section[block_of(place), columns] += (factor * lift_first[group]) * both
-
-    def advance(trace, thrice):
-        return 0.5 * field[...] + 0.5 * (section[...] + inner_slope(thrice, trace))
-
-    basis = first_basis()
+            shifted[block_of(low), :] = by_axis(*[traces[source] for source in sources[low]])
+        return fold(inner + dot(jnp.concatenate(split(shifted[...]), axis=1), lifts[...]))
+
+    def combinations(half):
+        plain, once, square_of = [
+            pair_of(matrix[2 * half : 2 * half + 2])
+            for matrix in (basis, basis @ interior, basis @ interior @ interior)
+        ]
+        step = first_scale
+        return (
+            mix(plain),
+            mix([2.0 * (p + step * o) for p, o in zip(plain, once)]),
+            mix([p + step * (o + 0.5 * step * q) for p, o, q in zip(plain, once, square_of)]),
+        )
+
+    def edge_at(stage, low):
+        edge = edge_in[stage, low % (LOW // 2)]
+        turned = swap(edge)
+        return halves(edge, turned) if low < LOW // 2 else halves(turned, edge)
+
+    pack(1, mix([first_scale * part for part in pair_of([right @ interior] * 2)]))
 
     def exchange(source, target, half, send_sem, recv_sem):
         copies = []
@@ -407,49 +424,48 @@
         target[half, me] = source[half, me]
         return copies
 
-    def to_owners(half):
+    def to_owners(half, advanced):
+        parts = blocks(advanced)
         for pair in range(LOW // 2):
-            blocks = []
-            for group in range(2):
-                columns = slice(128 * group, 128 * (group + 1))
-                even = section[block_of(2 * pair), columns]
-                odd = section[block_of(2 * pair + 1), columns]
-                blocks += [halves(even, swap(odd)), halves(swap(even), odd)]
-            turned = [
-                sum(float(basis[row, first]) * blocks[first] for first in range(4))
-                for row in (2 * half, 2 * half + 1)
-            ]
+            even, odd = parts[2 * pair], parts[2 * pair + 1]
             into = slice(128 * pair, 128 * (pair + 1))
-            hi, lo = split(jnp.concatenate(turned))
+            hi, lo = split(jnp.concatenate([halves(even, swap(odd)), halves(swap(even), odd)]))
             rows[half, :128, into] = hi
             rows[half, 128:, into] = lo
         both = dot_nt(h_hi, rows[half])
-        whole = both[:, :128] + both[:, 128:] + dot_nt(h_lo, rows[half, :128])
+        whole = fold(both) + dot_nt(h_lo, rows[half, :128])
         sent[half] = whole.reshape(sent.shape[1:])
         return exchange(sent, got, half, there_send, there_recv)
 
-    section[...] = field[...] + inner_slope(thrice, trace)
-    inside[...] = section[...]
-    thrice = triple(*split(section[...]))
-    trace = dot(thrice, trace_v[...])
-    for low in range(LOW // 2):
-        edge_out[1, low] = pack(trace[:, :128], low)
-    section[...] = advance(trace, thrice)
-    edge_copy.wait()
-    for low in range(LOW // 2):
-        edge_out[1, low] += edge_factor * edge_in[0, low]
-    edge_copy = send_edge(1)
+    def pass_edge():
+        first_edge.wait()
+        for low in range(LOW // 2):
+            edge_out[1, low] += (first_scale * RIGHT_LEFT) * edge_in[0, low]
+        second_edge.start()
+
+    trace_copy.wait()
+    y, m, u = combinations(0)
+    advanced = u + 0.5 * others_step(m + others_step(y))
     hier_copy.wait()
     h_hi, h_lo = hier_v[kind, 0], hier_v[kind, 1]
-    there = [to_owners(0)]
-
-    section[...] = inside[...]
-    add_edge(0, 1.0)
-    thrice = triple(*split(section[...]))
-    section[...] = advance(dot(thrice, trace_v[...]), thrice)
-    edge_copy.wait()
-    add_edge(1, 0.5)
-    there.append(to_owners(1))
+    there = [to_owners(0, advanced)]
+
+    pass_edge()
+    y, m, u = combinations(1)
+    bent = basis @ interior @ left
+    straight = float(basis[2] @ left)
+    to_m = jnp.where(left_half[:1], 2.0 * straight * first_scale, 0.0)
+    to_u = first_scale * jnp.where(
+        left_half[:1],
+        straight + 0.5 * float(bent[2]) * first_scale,
+        0.5 * float(bent[3]) * first_scale,
+    )
+    to_u2 = jnp.where(left_half[:1], 0.5 * straight * first_scale, 0.0)
+    edges = jnp.concatenate([edge_at(0, low) for low in range(LOW)], axis=0)
+    plane[...] = u + to_u * edges + 0.5 * others_step(m + to_m * edges + others_step(y))
+    second_edge.wait()
+    edges = jnp.concatenate([edge_at(1, low) for low in range(LOW)], axis=0)
+    there.append(to_owners(1, plane[...] + to_u2 * edges))
 
     coefs_copy.wait()
 
@@ -496,7 +512,7 @@
             part = slice(8 * quarter, 8 * (quarter + 1))
             hi, lo = split(got[half, :, part, :].reshape(8 * comps, 128))
             both = dot(match[...], jnp.concatenate([hi, lo], axis=1))
-            back[half, :, part, :] = (both[:, :128] + both[:, 128:]).reshape(comps, 8, 128)
+            back[half, :, part, :] = fold(both).reshape(comps, 8, 128)
         homeward.append(exchange(back, home, half, back_send, back_recv))
 
     for half in range(2):
@@ -508,10 +524,9 @@
         for pair in range(LOW // 2):
             into = slice(128 * pair, 128 * (pair + 1))
             upper, lower = plain[:64, into], plain[64:, into]
-            section[block_of(2 * pair), :128] = halves(upper, swap(lower))
-            section[block_of(2 * pair + 1), :128] = halves(swap(upper), lower)
-        both = dot(onehot[...], jnp.concatenate(split(section[:, :128]), axis=1))
-        turned = both[:, :128] + both[:, 128:]
+            plane[block_of(2 * pair), :] = halves(upper, swap(lower))
+            plane[block_of(2 * pair + 1), :] = halves(swap(upper), lower)
+        turned = fold(dot(onehot[...], jnp.concatenate(split(plane[...]), axis=1)))
         swapped = swap(turned)
         for group in range(2):
             near = [float(basis[2 * half + k, 2 * group + k]) for k in range(2)]
@@ -550,14 +565,13 @@
             pltpu.VMEM(hier.shape, BF16),
             pltpu.VMEM((GRID, GRID), BF16),
             pltpu.VMEM((8 * comps, 8 * comps), BF16),
-            pltpu.VMEM((3 * COEF, COEF), BF16),
-            pltpu.VMEM((3 * COEF, COEF), BF16),
+            pltpu.VMEM((COEF, COEF), BF16),
+            pltpu.VMEM((COEF, COEF), BF16),
+            pltpu.VMEM((GRID, COEF), F32),
             pltpu.VMEM((GRID, COEF), F32),
             pltpu.VMEM((2 * LOW, PLACES, 128), F32),
-            pltpu.VMEM((3 * LOW, PLACES, 128), F32),
-            pltpu.VMEM((GRID, COEF), F32),
-            pltpu.VMEM((GRID, COEF), F32),
-            pltpu.VMEM((GRID, COEF), F32),
+            pltpu.VMEM((GRID, 128), F32),
+            pltpu.VMEM((GRID, 128), F32),
             pltpu.VMEM((2, LOW // 2, PLACES, 128), F32),
             pltpu.VMEM((2, LOW // 2, PLACES, 128), F32),
             pltpu.VMEM((2, 2 * 128, GRID), BF16),

time: 43.2 us -> 40.9 us (0.947)
  Pallas kernels: 41.2 us -> 38.9 us
    pallas_call x1, Pallas kernels: 41.2 us -> 38.9 us  [on_device(): pl.pallas_call(functools.partial(kernel, comps, shards), out_shape=jax.Sh...]
where the time goes in v3:
time: 40.9 us; the launch traced here: 40.8 us
  Pallas kernels  38.9 us (95%)
  local copies, waits for them, and re-layouts  1.87 us (5%)
    pallas_call x1, Pallas kernels, on_device(): pl.pallas_call(functools.partial(kernel, comps, shards), out_shape=jax.Sh...  38.9 us
    unnamed x1, local copies, waits for them, and re-layouts  1.87 us

profile of v3, /device:TPU:2, one launch (start us, length us, event | category | flops | bytes accessed | tf_op | source)
XLA Modules:
  0.0 40.8 jit_solution(12368018068331749145)
XLA Ops:
  0.0 38.9 %combine.1 = f32[1,1,512,256]{3,2,1,0:T(8,128)} custom-call(s32[3,16]{1,0:T(4,128)} %bitcast.1, s32[16]{0:T(128)} %coefs_hbm.1, f32[4]{0:T(128)} %velocity_hbm.1, f32[1,1,512,256]{3,2,1,0:T(8,128)} %x_hbm.1, f32[3,128,128]{2,1,0:T(8,128)} %constant.8.clone.stiff_hbm, f32[128,128]{1,0:T(8,128)} %constant.9.clone.lift_hbm, ...), custom_call_target="tpu_custom_call" | custom-call | tf_op jit(solution)/shard_map/combine/pallas_call | solution.py:552
  38.9 1.9 %copy.10 = f32[1,1,512,256]{3,2,1,0:T(8,128)} copy(f32[1,1,512,256]{3,2,1,0:T(8,128)} %combine.1) | data formatting | bytes 1048576

commit v4 on v3

--- a/solution.py
+++ b/solution.py
@@ -21,8 +21,8 @@
 MESH = pl.DeviceIdType.MESH
 
 courant = 0.1
-VMEM_LIMIT = 62 * 2**20
-ORDER = (8, 4, 12, 5, 11, 3, 13, 6, 10, 2, 14, 7, 9, 1, 15)
+VMEM_LIMIT = 48 * 2**20
+ORDER = (4, 5, 3, 6, 2, 7, 1, 12, 13, 11, 14, 10, 15, 9, 8)
 RIGHT_LEFT = float(sum((-1) ** order * (2 * order + 1) / 2.0 for order in range(4)))
 
 
@@ -225,7 +225,6 @@
         pl.semaphore_signal(
             barrier, inc=1, device_id={"comp": lax.rem(me + step, comps)}, device_id_type=MESH
         )
-    pl.semaphore_signal(barrier, inc=1, device_id={"shard": ahead}, device_id_type=MESH)
     pl.semaphore_signal(barrier, inc=1, device_id={"shard": behind}, device_id_type=MESH)
 
     levels_copy.wait()
@@ -324,7 +323,7 @@
             edge_out[stage, low] = halves(parts[low], parts[low + LOW // 2])
 
     pack(0, mix(pair_of([right, right])))
-    pl.semaphore_wait(barrier, comps + 1)
+    pl.semaphore_wait(barrier, comps)
     first_edge, second_edge = edge_copy(0), edge_copy(1)
     first_edge.start()
 
@@ -526,20 +525,23 @@
             upper, lower = plain[:64, into], plain[64:, into]
             plane[block_of(2 * pair), :] = halves(upper, swap(lower))
             plane[block_of(2 * pair + 1), :] = halves(swap(upper), lower)
-        turned = fold(dot(onehot[...], jnp.concatenate(split(plane[...]), axis=1)))
-        swapped = swap(turned)
-        for group in range(2):
-            near = [float(basis[2 * half + k, 2 * group + k]) for k in range(2)]
-            far = [float(basis[2 * half + 1 - k, 2 * group + k]) for k in range(2)]
-            part = (
-                jnp.where(left_half[:1], near[0], near[1]) * turned
-                + jnp.where(left_half[:1], far[0], far[1]) * swapped
-            )
-            columns = slice(128 * group, 128 * (group + 1))
-            if half == 0:
-                out_ref[0, 0, :, columns] = part
-            else:
-                out_ref[0, 0, :, columns] += part
+        pair = jnp.concatenate(split(plane[...]), axis=1)
+        for part in range(4):
+            cells = slice(128 * part, 128 * (part + 1))
+            turned = fold(dot(onehot[cells, :], pair))
+            swapped = swap(turned)
+            for group in range(2):
+                near = [float(basis[2 * half + k, 2 * group + k]) for k in range(2)]
+                far = [float(basis[2 * half + 1 - k, 2 * group + k]) for k in range(2)]
+                value = (
+                    jnp.where(left_half[:1], near[0], near[1]) * turned
+                    + jnp.where(left_half[:1], far[0], far[1]) * swapped
+                )
+                columns = slice(128 * group, 128 * (group + 1))
+                if half == 0:
+                    out_ref[0, 0, cells, columns] = value
+                else:
+                    out_ref[0, 0, cells, columns] += value
 
 
 def on_device(modal_coefs, comp_levels, comp_coefs, velocity):
@@ -551,7 +553,7 @@
     exchanged = pltpu.VMEM((2, comps, GRID // comps, 128), F32)
     return pl.pallas_call(
         functools.partial(kernel, comps, shards),
-        out_shape=jax.ShapeDtypeStruct(modal_coefs.shape, F32),
+        out_shape=pltpu.VMEM(modal_coefs.shape, F32),
         in_specs=[anywhere] * 8,
         out_specs=pl.BlockSpec(memory_space=pltpu.VMEM),
         scratch_shapes=[
@@ -592,14 +594,19 @@
         ),
         name="combine",
     )(
-        comp_levels.T,
-        comp_coefs,
-        velocity,
-        modal_coefs,
-        jnp.asarray(stiff),
-        jnp.asarray(lift),
-        jnp.asarray(trace),
-        jnp.asarray(hier),
+        *[
+            pltpu.with_memory_space_constraint(array, pltpu.HBM)
+            for array in (
+                comp_levels.T,
+                comp_coefs,
+                velocity,
+                modal_coefs,
+                jnp.asarray(stiff),
+                jnp.asarray(lift),
+                jnp.asarray(trace),
+                jnp.asarray(hier),
+            )
+        ]
     )
 
 

time: 40.9 us -> 38.4 us (0.939)
  Pallas kernels: 38.9 us -> 37.2 us
  local copies, waits for them, and re-layouts: 1.87 us -> 0.8 us
    pallas_call x1, Pallas kernels: 38.9 us -> 37.2 us  [on_device(): pl.pallas_call(functools.partial(kernel, comps, shards), out_shape=pltpu....]
    unnamed x1, local copies, waits for them, and re-layouts: 1.87 us -> 0.8 us
where the time goes in v4:
time: 38.4 us; the launch traced here: 38 us
  Pallas kernels  37.2 us (97%)
  local copies, waits for them, and re-layouts  0.8 us (2%)
    pallas_call x1, Pallas kernels, on_device(): pl.pallas_call(functools.partial(kernel, comps, shards), out_shape=pltpu....  37.2 us
    unnamed x1, local copies, waits for them, and re-layouts  0.8 us

profile of v4, /device:TPU:2, one launch (start us, length us, event | category | flops | bytes accessed | tf_op | source)
XLA Modules:
  0.0 38.0 jit_solution(17034699165398588896)
XLA Ops:
  0.0 37.2 %combine.1 = f32[1,1,512,256]{3,2,1,0:T(8,128)S(1)} custom-call(s32[3,16]{1,0:T(4,128)} %bitcast.1, s32[16]{0:T(128)} %coefs_hbm.1, f32[4]{0:T(128)} %velocity_hbm.1, f32[1,1,512,256]{3,2,1,0:T(8,128)} %x_hbm.1, f32[3,128,128]{2,1,0:T(8,128)} %constant.8.clone.stiff_hbm, f32[128,128]{1,0:T(8,128)} %constant.9.clone.lift_hbm, ...), custom_call_target="tpu_custom_call" | custom-call | tf_op jit(solution)/shard_map/combine/pallas_call | solution.py:554
  37.2 0.8 %copy.10 = f32[1,1,512,256]{3,2,1,0:T(8,128)} copy(f32[1,1,512,256]{3,2,1,0:T(8,128)S(1)} %combine.1) | data formatting | bytes 1048576

commit v5 on v4

--- a/solution.py
+++ b/solution.py
@@ -406,7 +406,7 @@
 
     pack(1, mix([first_scale * part for part in pair_of([right @ interior] * 2)]))
 
-    def exchange(source, target, half, send_sem, recv_sem):
+    def exchange(source, target, half, send_sem, recv_sem, turns=()):
         copies = []
         for step in ORDER:
             other = lax.rem(me + step, comps)
@@ -418,10 +418,15 @@
                 device_id={"comp": other},
                 device_id_type=MESH,
             )
-            copy.start()
-            copies.append(copy)
+            copies.append((copy, lax.rem(other, 8)))
+        for first, last in turns or [(0, 8)]:
+            for copy, height in copies:
+                if turns:
+                    pl.when((height >= first) & (height < last))(copy.start)
+                else:
+                    copy.start()
         target[half, me] = source[half, me]
-        return copies
+        return [copy for copy, _ in copies]
 
     def to_owners(half, advanced):
         parts = blocks(advanced)
@@ -512,7 +517,7 @@
             hi, lo = split(got[half, :, part, :].reshape(8 * comps, 128))
             both = dot(match[...], jnp.concatenate([hi, lo], axis=1))
             back[half, :, part, :] = fold(both).reshape(comps, 8, 128)
-        homeward.append(exchange(back, home, half, back_send, back_recv))
+        homeward.append(exchange(back, home, half, back_send, back_recv, [(0, 2), (2, 8)] if half else ()))
 
     for half in range(2):
         for copy in homeward[half]:

time: 38.4 us -> 37.7 us (0.982)
  Pallas kernels: 37.2 us -> 36.5 us
    pallas_call x1, Pallas kernels: 37.2 us -> 36.5 us  [on_device(): pl.pallas_call(functools.partial(kernel, comps, shards), out_shape=pltpu....]
where the time goes in v5:
time: 37.7 us; the launch traced here: 37.3 us
  Pallas kernels  36.5 us (97%)
  local copies, waits for them, and re-layouts  0.8 us (2%)
    pallas_call x1, Pallas kernels, on_device(): pl.pallas_call(functools.partial(kernel, comps, shards), out_shape=pltpu....  36.5 us
    unnamed x1, local copies, waits for them, and re-layouts  0.8 us

profile of v5, /device:TPU:2, one launch (start us, length us, event | category | flops | bytes accessed | tf_op | source)
XLA Modules:
  0.0 37.3 jit_solution(13012908289598509123)
XLA Ops:
  0.0 36.5 %combine.1 = f32[1,1,512,256]{3,2,1,0:T(8,128)S(1)} custom-call(s32[3,16]{1,0:T(4,128)} %bitcast.1, s32[16]{0:T(128)} %coefs_hbm.1, f32[4]{0:T(128)} %velocity_hbm.1, f32[1,1,512,256]{3,2,1,0:T(8,128)} %x_hbm.1, f32[3,128,128]{2,1,0:T(8,128)} %constant.8.clone.stiff_hbm, f32[128,128]{1,0:T(8,128)} %constant.9.clone.lift_hbm, ...), custom_call_target="tpu_custom_call" | custom-call | tf_op jit(solution)/shard_map/combine/pallas_call | solution.py:559
  36.5 0.8 %copy.10 = f32[1,1,512,256]{3,2,1,0:T(8,128)} copy(f32[1,1,512,256]{3,2,1,0:T(8,128)S(1)} %combine.1) | data formatting | bytes 1048576

commit v6 on v5

--- a/solution.py
+++ b/solution.py
@@ -283,50 +283,6 @@
     def blocks(values):
         return [values[block_of(low), :] for low in range(LOW)]
 
-    x_copy.wait()
-    hi, lo = split(x_v[...])
-    now = dot(onehot[...], hi) + dot(onehot[...], lo)
-    field[...] = now
-    other[:, :128] = swap(now[:, :128])
-    other[:, 128:] = swap(now[:, 128:])
-
-    basis = first_basis()
-    interior, right, left, _ = line_tables()
-
-    def pair_of(rows_of):
-        return [
-            jnp.where(left_half[:1], float(rows_of[0][first]), float(rows_of[1][second]))
-            for first, second in ((0, 1), (1, 0), (2, 3), (3, 2))
-        ]
-
-    def mix(factors):
-        return (
-            factors[0] * field[:, :128]
-            + factors[1] * other[:, :128]
-            + factors[2] * field[:, 128:]
-            + factors[3] * other[:, 128:]
-        )
-
-    def edge_copy(stage):
-        return pltpu.make_async_remote_copy(
-            src_ref=edge_out.at[stage],
-            dst_ref=edge_in.at[stage],
-            send_sem=edge_send.at[stage],
-            recv_sem=edge_recv.at[stage],
-            device_id={"shard": ahead},
-            device_id_type=MESH,
-        )
-
-    def pack(stage, values):
-        parts = blocks(values)
-        for low in range(LOW // 2):
-            edge_out[stage, low] = halves(parts[low], parts[low + LOW // 2])
-
-    pack(0, mix(pair_of([right, right])))
-    pl.semaphore_wait(barrier, comps)
-    first_edge, second_edge = edge_copy(0), edge_copy(1)
-    first_edge.start()
-
     velocity_copy.wait()
     reach = None
     for comp in range(comps):
@@ -352,6 +308,50 @@
         jnp.concatenate([*scale_rows, jnp.zeros((32, 128), F32)], axis=0) * lift_v[...]
     )
 
+    x_copy.wait()
+    hi, lo = split(x_v[...])
+    now = dot(onehot[...], hi) + dot(onehot[...], lo)
+    field[...] = now
+    other[:, :128] = swap(now[:, :128])
+    other[:, 128:] = swap(now[:, 128:])
+
+    basis = first_basis()
+    interior, right, left, _ = line_tables()
+
+    def pair_of(rows_of):
+        return [
+            jnp.where(left_half[:1], float(rows_of[0][first]), float(rows_of[1][second]))
+            for first, second in ((0, 1), (1, 0), (2, 3), (3, 2))
+        ]
+
+    def mix(factors):
+        return (
+            factors[0] * field[:, :128]
+            + factors[1] * other[:, :128]
+            + factors[2] * field[:, 128:]
+            + factors[3] * other[:, 128:]
+        )
+
+    def edge_copy(stage):
+        return pltpu.make_async_remote_copy(
+            src_ref=edge_out.at[stage],
+            dst_ref=edge_in.at[stage],
+            send_sem=edge_send.at[stage],
+            recv_sem=edge_recv.at[stage],
+            device_id={"shard": ahead},
+            device_id_type=MESH,
+        )
+
+    def pack(stage, values):
+        parts = blocks(values)
+        for low in range(LOW // 2):
+            edge_out[stage, low] = halves(parts[low], parts[low + LOW // 2])
+
+    pack(0, mix(pair_of([right, right])))
+    pl.semaphore_wait(barrier, comps)
+    first_edge, second_edge = edge_copy(0), edge_copy(1)
+    first_edge.start()
+
     def behind_of(low, axis):
         digits = list(low_digits(jnp.int32(low)))
         rise = (rise1, rise2, rise3)[axis]
@@ -404,7 +404,6 @@
         turned = swap(edge)
         return halves(edge, turned) if low < LOW // 2 else halves(turned, edge)
 
-    pack(1, mix([first_scale * part for part in pair_of([right @ interior] * 2)]))
 
     def exchange(source, target, half, send_sem, recv_sem, turns=()):
         copies = []
@@ -428,6 +427,18 @@
         target[half, me] = source[half, me]
         return [copy for copy, _ in copies]
 
+    odd_height = lax.rem(me, 2) == 1
+
+    def one_copy(half, other, slot):
+        return pltpu.make_async_remote_copy(
+            src_ref=sent.at[half, other],
+            dst_ref=got.at[half, me],
+            send_sem=there_send.at[half, slot],
+            recv_sem=there_recv.at[half, slot],
+            device_id={"comp": other},
+            device_id_type=MESH,
+        )
+
     def to_owners(half, advanced):
         parts = blocks(advanced)
         for pair in range(LOW // 2):
@@ -436,10 +447,22 @@
             hi, lo = split(jnp.concatenate([halves(even, swap(odd)), halves(swap(even), odd)]))
             rows[half, :128, into] = hi
             rows[half, 128:, into] = lo
-        both = dot_nt(h_hi, rows[half])
-        whole = fold(both) + dot_nt(h_lo, rows[half, :128])
-        sent[half] = whole.reshape(sent.shape[1:])
-        return exchange(sent, got, half, there_send, there_recv)
+        copies = []
+        for side in range(2):
+            wing = jnp.where((me < comps // 2) ^ odd_height, side, 1 - side) * (comps // 2)
+            of_wing = pl.ds(pl.multiple_of(wing * (GRID // comps), GRID // 2), GRID // 2)
+            both = dot_nt(hier_v[kind, 0, of_wing, :], rows[half])
+            whole = fold(both) + dot_nt(hier_v[kind, 1, of_wing, :], rows[half, :128])
+            sent[half, pl.ds(wing, comps // 2)] = whole.reshape(comps // 2, GRID // comps, 128)
+            cross = jnp.where(odd_height, 1 - side, side)
+            for step in (4, 5, 3, 6, 2, 7, 1):
+                other = lax.rem(me + 8 * cross, comps) // 8 * 8 + lax.rem(me + step, 8)
+                copies.append(one_copy(half, other, 8 * cross + step))
+                copies[-1].start()
+        copies.append(one_copy(half, lax.rem(me + 8, comps), 8))
+        copies[-1].start()
+        got[half, me] = sent[half, me]
+        return copies
 
     def pass_edge():
         first_edge.wait()
@@ -454,6 +477,7 @@
     h_hi, h_lo = hier_v[kind, 0], hier_v[kind, 1]
     there = [to_owners(0, advanced)]
 
+    pack(1, mix([first_scale * part for part in pair_of([right @ interior] * 2)]))
     pass_edge()
     y, m, u = combinations(1)
     bent = basis @ interior @ left

time: 37.7 us -> 37.6 us (level)
  no operation moved by 1% of the time
where the time goes in v6:
time: 37.6 us; the launch traced here: 37.3 us
  Pallas kernels  36.5 us (97%)
  local copies, waits for them, and re-layouts  0.8 us (2%)
    pallas_call x1, Pallas kernels, on_device(): pl.pallas_call(functools.partial(kernel, comps, shards), out_shape=pltpu....  36.5 us
    unnamed x1, local copies, waits for them, and re-layouts  0.8 us

profile of v6, /device:TPU:2, one launch (start us, length us, event | category | flops | bytes accessed | tf_op | source)
XLA Modules:
  0.0 37.3 jit_solution(9372414304682327143)
XLA Ops:
  0.0 36.5 %combine.1 = f32[1,1,512,256]{3,2,1,0:T(8,128)S(1)} custom-call(s32[3,16]{1,0:T(4,128)} %bitcast.1, s32[16]{0:T(128)} %coefs_hbm.1, f32[4]{0:T(128)} %velocity_hbm.1, f32[1,1,512,256]{3,2,1,0:T(8,128)} %x_hbm.1, f32[3,128,128]{2,1,0:T(8,128)} %constant.8.clone.stiff_hbm, f32[128,128]{1,0:T(8,128)} %constant.9.clone.lift_hbm, ...), custom_call_target="tpu_custom_call" | custom-call | tf_op jit(solution)/shard_map/combine/pallas_call | solution.py:583
  36.5 0.8 %copy.10 = f32[1,1,512,256]{3,2,1,0:T(8,128)} copy(f32[1,1,512,256]{3,2,1,0:T(8,128)S(1)} %combine.1) | data formatting | bytes 1048576

commit v7 on v6

--- a/solution.py
+++ b/solution.py
@@ -478,8 +478,10 @@
     there = [to_owners(0, advanced)]
 
     pack(1, mix([first_scale * part for part in pair_of([right @ interior] * 2)]))
-    pass_edge()
+    pl.when(lax.rem(spot, 2) == 1)(pass_edge)
     y, m, u = combinations(1)
+    plane[...] = m + others_step(y)
+    pl.when(lax.rem(spot, 2) == 0)(pass_edge)
     bent = basis @ interior @ left
     straight = float(basis[2] @ left)
     to_m = jnp.where(left_half[:1], 2.0 * straight * first_scale, 0.0)
@@ -490,7 +492,7 @@
     )
     to_u2 = jnp.where(left_half[:1], 0.5 * straight * first_scale, 0.0)
     edges = jnp.concatenate([edge_at(0, low) for low in range(LOW)], axis=0)
-    plane[...] = u + to_u * edges + 0.5 * others_step(m + to_m * edges + others_step(y))
+    plane[...] = u + to_u * edges + 0.5 * others_step(plane[...] + to_m * edges)
     second_edge.wait()
     edges = jnp.concatenate([edge_at(1, low) for low in range(LOW)], axis=0)
     there.append(to_owners(1, plane[...] + to_u2 * edges))

time: 37.6 us -> 37.6 us (level)
  no operation moved by 1% of the time
where the time goes in v7:
time: 37.6 us; the launch traced here: 37.3 us
  Pallas kernels  36.5 us (97%)
  local copies, waits for them, and re-layouts  0.8 us (2%)
    pallas_call x1, Pallas kernels, on_device(): pl.pallas_call(functools.partial(kernel, comps, shards), out_shape=pltpu....  36.5 us
    unnamed x1, local copies, waits for them, and re-layouts  0.8 us

profile of v7, /device:TPU:2, one launch (start us, length us, event | category | flops | bytes accessed | tf_op | source)
XLA Modules:
  0.0 37.3 jit_solution(10032428155146076253)
XLA Ops:
  0.0 36.5 %combine.1 = f32[1,1,512,256]{3,2,1,0:T(8,128)S(1)} custom-call(s32[3,16]{1,0:T(4,128)} %bitcast.1, s32[16]{0:T(128)} %coefs_hbm.1, f32[4]{0:T(128)} %velocity_hbm.1, f32[1,1,512,256]{3,2,1,0:T(8,128)} %x_hbm.1, f32[3,128,128]{2,1,0:T(8,128)} %constant.8.clone.stiff_hbm, f32[128,128]{1,0:T(8,128)} %constant.9.clone.lift_hbm, ...), custom_call_target="tpu_custom_call" | custom-call | tf_op jit(solution)/shard_map/combine/pallas_call | solution.py:585
  36.5 0.8 %copy.10 = f32[1,1,512,256]{3,2,1,0:T(8,128)} copy(f32[1,1,512,256]{3,2,1,0:T(8,128)S(1)} %combine.1) | data formatting | bytes 1048576
